TPU v7x, 32 devices: a whole 2x2x4 slice. The times are simulated.
32 devices in a mesh: coarse: 8 (over y, x, core), fan: 4 (over z).
Axes of the slice: x: 2, y: 2, z: 4, core: 2. Of those that a mesh axis runs over, the one named last changes fastest.
Arguments:
- right_side: float32 [512, 64, 128], P(('coarse', 'fan')), may hold values from -6 to 6
- fine_matrix: bfloat16 [512, 7, 64, 64], P(('coarse', 'fan')), as said below
- fine_columns: int32 [512, 7], P(('coarse', 'fan')), may hold values from 0 to 23, as said below
- fine_inverse: bfloat16 [512, 64, 64], P(('coarse', 'fan')), as said below
- prolong: bfloat16 [512, 64, 64], P(('coarse', 'fan')), may hold values from -0.75 to 0.75
- aggregate: int32 [512], P(('coarse', 'fan')), may hold values from 0 to 1, as said below
- coarse_matrix: bfloat16 [64, 7, 64, 64], P('coarse'), as said below
- coarse_columns: int32 [64, 7], P('coarse'), may hold values from 0 to 11, as said below
- coarse_inverse: bfloat16 [64, 64, 64], P('coarse'), as said below
Outputs:
- solution: float32 [512, 64, 128], P(('coarse', 'fan'))
- residual_out: float32 [512, 64, 128], P(('coarse', 'fan'))
Inputs may be any that keep to these rules, and one draw needn't show every extreme that they name: `fine_columns`: slot 0 names the row itself; every entry lies within 4 of the row's own position plus 4. `coarse_columns`: slot 0 names the row itself. `aggregate`: every value is named by exactly 8 rows of each device. `fine_matrix`: slot 0 is the diagonal block. `coarse_matrix`: slot 0 is the diagonal block. `fine_inverse`: approximates the inverse of the fine diagonal block. `coarse_inverse`: approximates the inverse of the coarse diagonal block.
All inputs are finite; a program needn't handle non-finite values.
Results may differ from a plain program's by a relative error of at most 0.02.
Values sent between devices are 32-bit elements; how exact they have to be, the bound alone decides.
A program may use at most 64 MiB of HBM per device.

v0:
```python
import functools

import jax
import jax.numpy as jnp
from jax import lax
from jax.experimental import pallas as pl
from jax.experimental.pallas import tpu as pltpu
from jax.sharding import PartitionSpec as P

H = 4
HC = 2
CSWEEPS = 4
EXCHANGES = 8
relaxation = 0.6
MESH = pl.DeviceIdType.MESH
F32 = jnp.float32
BF16 = jnp.bfloat16


def dot(a, b):
    return jnp.dot(a, b, preferred_element_type=F32)


def two_term(matrix, halves):
    both = dot(matrix, halves)
    width = both.shape[1] // 2
    return both[:, :width] + both[:, width:]


def kernel(
    coarse_size, fan_size,
    b_ref, a_ref, acol_ref, d_ref, p_ref, agg_ref, c_ref, ccol_ref, ci_ref,
    x_ref, res_ref,
    ad, dd, pd, ptd, cd, cid, xhl, ehl, e_ref, rhs, edge_out, halo_in,
    ce_out, ce_in, pe_out, pe_in,
    fs_sem, fr_sem, gs_sem, gr_sem, cs_sem, cr_sem, ps_sem, pr_sem,
):
    rows, slots, B, _ = a_ref.shape
    R = b_ref.shape[1]
    grows = c_ref.shape[0]
    rc = grows // fan_size
    HB = H * B
    CB = HC * B
    PB = rc * B
    ng = rows // H
    c = lax.axis_index("coarse")
    f = lax.axis_index("fan")
    place = c * fan_size + f
    before, after = place - 1, place + 1
    fine_to = (
        (before // fan_size, before % fan_size),
        (after // fan_size, after % fan_size),
    )
    fine_has = (place > 0, place < coarse_size * fan_size - 1)
    coarse_to = ((c - 1, f), (c + 1, f))
    coarse_has = (c > 0, c < coarse_size - 1)
    peers = [(c, (f + k) % fan_size) for k in range(1, fan_size)]

    barrier = pltpu.get_barrier_semaphore()
    for has, to in zip(fine_has + coarse_has, fine_to + coarse_to):
        @pl.when(has)
        def _():
            pl.semaphore_signal(barrier, inc=1, device_id=to, device_id_type=MESH)
    for to in peers:
        pl.semaphore_signal(barrier, inc=1, device_id=to, device_id_type=MESH)

    half = (lax.broadcasted_iota(jnp.int32, (1, 2 * B), 1) >= B).astype(jnp.int32)

    def build(count, blocks, names, pairs, dst):
        def row(r, carry):
            doubled = []
            for block in blocks(r):
                wide = block.astype(F32)
                doubled.append(jnp.concatenate([wide, wide], axis=1))
            named = names(r)
            for p in range(pairs):
                at = half + 2 * p
                total = None
                for block, name in zip(doubled, named):
                    term = jnp.where(at == name, block, 0.0)
                    total = term if total is None else total + term
                dst[pl.ds(pl.multiple_of(r * B, B), B), 2 * p * B:(2 * p + 2) * B] = total.astype(BF16)
            return carry

        lax.fori_loop(0, count, row, 0)

    def put_halves(ref, start, value):
        high = value.astype(BF16)
        low = (value - high.astype(F32)).astype(BF16)
        n = value.shape[0]
        ref[start:start + n, :R] = high
        ref[start:start + n, R:] = low

    def fine_copy(t, d):
        return pltpu.make_async_remote_copy(
            src_ref=edge_out.at[t, d], dst_ref=halo_in.at[t, 1 - d],
            send_sem=fs_sem.at[t, d], recv_sem=fr_sem.at[t, 1 - d],
            device_id=fine_to[d], device_id_type=MESH)

    def fine_send(t, d, value):
        edge_out[t, d] = value

        @pl.when(fine_has[d])
        def _():
            fine_copy(t, d).start()

    def fine_wait(t, d, slot):
        @pl.when(fine_has[d])
        def _():
            pltpu.make_async_remote_copy(
                src_ref=edge_out.at[t, 1 - d], dst_ref=halo_in.at[t, d],
                send_sem=fs_sem.at[t, 1 - d], recv_sem=fr_sem.at[t, d],
                device_id=fine_to[d], device_id_type=MESH).wait_recv()
            put_halves(xhl.at[slot], d * (rows + H) * B, halo_in[t, d])

    def coarse_copy(s, d):
        return pltpu.make_async_remote_copy(
            src_ref=ce_out.at[s, d], dst_ref=ce_in.at[s, 1 - d],
            send_sem=cs_sem.at[s, d], recv_sem=cr_sem.at[s, 1 - d],
            device_id=coarse_to[d], device_id_type=MESH)

    def coarse_sent(d, last):
        if not last:
            return coarse_has[d]
        return coarse_has[d] & (f == (fan_size - 1 if d == 0 else 0))

    def coarse_came(d, last):
        if not last:
            return coarse_has[d]
        return coarse_has[d] & (f == (0 if d == 0 else fan_size - 1))

    def coarse_send(s, d, value, last):
        ce_out[s, d] = value

        @pl.when(coarse_sent(d, last))
        def _():
            coarse_copy(s, d).start()

    def coarse_wait(s, d, last):
        @pl.when(coarse_came(d, last))
        def _():
            pltpu.make_async_remote_copy(
                src_ref=ce_out.at[s, 1 - d], dst_ref=ce_in.at[s, d],
                send_sem=cs_sem.at[s, 1 - d], recv_sem=cr_sem.at[s, d],
                device_id=coarse_to[d], device_id_type=MESH).wait_recv()
            put_halves(ehl, d * (grows + HC) * B, ce_in[s, d])

    def edge_matrix_copy(d):
        return pltpu.make_async_remote_copy(
            src_ref=pe_out.at[d], dst_ref=pe_in.at[1 - d],
            send_sem=ps_sem.at[d], recv_sem=pr_sem.at[1 - d],
            device_id=fine_to[d], device_id_type=MESH)

    def group(g):
        return slice(g * HB, (g + 1) * HB)

    def step_of(g, residual):
        return relaxation * dot(dd[group(g), :], residual.astype(BF16))

    def set_group(g, value, slot, t):
        x_ref[group(g), :] = value
        put_halves(xhl.at[slot], (g + 1) * HB, value)
        if t is not None and g == 0:
            fine_send(t, 0, value)
        if t is not None and g == ng - 1:
            fine_send(t, 1, value)

    def residuals(slot, t, use):
        for g in range(1, ng - 1):
            use(g, b_ref[group(g), :] - two_term(ad[group(g), :], xhl[slot, g * HB:(g + 3) * HB, :]))
        low = b_ref[group(0), :] - two_term(ad[group(0), HB:], xhl[slot, HB:3 * HB, :])
        last = ng - 1
        high = b_ref[group(last), :] - two_term(
            ad[group(last), :2 * HB], xhl[slot, last * HB:(last + 2) * HB, :])
        if t is not None:
            fine_wait(t, 0, slot)
        use(0, low - two_term(ad[group(0), :HB], xhl[slot, :HB, :]))
        if t is not None:
            fine_wait(t, 1, slot)
        use(last, high - two_term(ad[group(last), 2 * HB:], xhl[slot, (last + 2) * HB:, :]))

    def sweep(slot, t_in, t_out):
        def use(g, residual):
            set_group(g, x_ref[group(g), :] + step_of(g, residual), 1 - slot, t_out)

        residuals(slot, t_in, use)
        return 1 - slot

    def relax_coarse(values):
        return [
            relaxation * dot(cid[g * HB:(g + 1) * HB, :], v.astype(BF16))
            for g, v in enumerate(values)
        ]

    cg = grows // H

    def correct(cycle, slot, t_in):
        pieces = []

        def use(g, residual):
            pieces.append(dot(ptd[:, group(g)], residual.astype(BF16)))

        residuals(slot, t_in, use)
        mine = pl.ds(pl.multiple_of(f * PB, PB), PB)
        rhs[cycle, mine, :] = functools.reduce(jnp.add, pieces)
        copies = []
        for k, to in enumerate(peers):
            copy = pltpu.make_async_remote_copy(
                src_ref=rhs.at[cycle, mine], dst_ref=rhs.at[cycle, mine],
                send_sem=gs_sem.at[cycle, k], recv_sem=gr_sem.at[cycle, k],
                device_id=to, device_id_type=MESH)
            copy.start()
            copies.append(copy)
        if cycle == 0:
            pe_out[0] = pd[:HB, :].astype(F32)
            pe_out[1] = pd[(ng - 1) * HB:, :].astype(F32)
            for d in range(2):
                @pl.when(fine_has[d])
                def _():
                    edge_matrix_copy(d).start()
        for k in range(fan_size - 1):
            theirs = pl.ds(pl.multiple_of(((f - k - 1 + fan_size) % fan_size) * PB, PB), PB)
            pltpu.make_async_remote_copy(
                src_ref=rhs.at[cycle, theirs], dst_ref=rhs.at[cycle, theirs],
                send_sem=gs_sem.at[cycle, k], recv_sem=gr_sem.at[cycle, k],
                device_id=peers[k], device_id_type=MESH).wait_recv()

        def publish(e, s, last):
            coarse_send(s, 0, e[0][:CB, :], last)
            coarse_send(s, 1, e[-1][HB - CB:, :], last)
            for g in range(cg):
                e_ref[group(g), :] = e[g]
                put_halves(ehl, CB + g * HB, e[g])

        s = cycle * CSWEEPS
        publish(relax_coarse([rhs[cycle, group(g), :] for g in range(cg)]), s, False)
        for step in range(1, CSWEEPS):
            own = [
                rhs[cycle, group(g), :]
                - two_term(cd[group(g), CB:CB + grows * B], ehl[CB:CB + grows * B, :])
                for g in range(cg)
            ]
            coarse_wait(s, 0, False)
            own = [v - two_term(cd[group(g), :CB], ehl[:CB, :]) for g, v in enumerate(own)]
            coarse_wait(s, 1, False)
            own = [
                v - two_term(cd[group(g), CB + grows * B:], ehl[CB + grows * B:, :])
                for g, v in enumerate(own)
            ]
            e = [e_ref[group(g), :] + v for g, v in enumerate(relax_coarse(own))]
            s = s + 1
            publish(e, s, step == CSWEEPS - 1)

        other = 1 - slot
        lifted = ehl[pl.ds(pl.multiple_of(CB + f * PB, PB), PB), :]
        for g in range(ng):
            set_group(g, x_ref[group(g), :] + two_term(pd[group(g), :], lifted), other, None)
        for d in range(2):
            if cycle == 0:
                @pl.when(fine_has[d])
                def _():
                    pltpu.make_async_remote_copy(
                        src_ref=pe_out.at[1 - d], dst_ref=pe_in.at[d],
                        send_sem=ps_sem.at[1 - d], recv_sem=pr_sem.at[d],
                        device_id=fine_to[d], device_id_type=MESH).wait_recv()
            coarse_wait(s, d, True)

            @pl.when(fine_has[d])
            def _():
                theirs = ehl[pl.ds(pl.multiple_of(CB + (f + 2 * d - 1) * PB, PB), PB), :]
                value = halo_in[t_in, d] + two_term(pe_in[d].astype(BF16), theirs)
                put_halves(xhl.at[other], d * (rows + H) * B, value)
        return other, copies

    build(rows, lambda r: [d_ref[r]], lambda r: [r % H], H // 2, dd)
    waits = (
        sum(h.astype(jnp.int32) for h in fine_has + coarse_has) + (fan_size - 1)
    )
    pl.semaphore_wait(barrier, waits)
    for g in (0, ng - 1) + tuple(range(1, ng - 1)):
        set_group(g, step_of(g, b_ref[group(g), :]), 0, 0)
    for d in range(2):
        @pl.when(jnp.logical_not(fine_has[d]))
        def _():
            for slot in range(2):
                at = d * (rows + H) * B
                xhl[slot, at:at + HB, :] = jnp.zeros((HB, 2 * R), BF16)

        @pl.when(jnp.logical_not(coarse_has[d]))
        def _():
            at = d * (grows + HC) * B
            ehl[at:at + CB, :] = jnp.zeros((CB, 2 * R), BF16)

    build(
        rows,
        lambda r: [a_ref[r, k] for k in range(slots)],
        lambda r: [acol_ref[r, k] - (r // H) * H for k in range(slots)],
        3 * H // 2, ad)
    build(rows, lambda r: [p_ref[r]], lambda r: [agg_ref[r]], rc // 2, pd)
    for g in range(ng):
        ptd[:, group(g)] = jnp.transpose(pd[group(g), :].astype(F32)).astype(BF16)
    build(
        grows,
        lambda r: [c_ref[r, k] for k in range(c_ref.shape[1])],
        lambda r: [ccol_ref[r, k] for k in range(c_ref.shape[1])],
        (grows + 2 * HC) // 2, cd)
    build(grows, lambda r: [ci_ref[r]], lambda r: [r % H], H // 2, cid)

    slot = sweep(0, 0, 1)
    slot, first = correct(0, slot, 1)
    slot = sweep(slot, None, 2)
    slot = sweep(slot, 2, 3)
    slot = sweep(slot, 3, 4)
    slot = sweep(slot, 4, 5)
    slot, second = correct(1, slot, 5)
    slot = sweep(slot, None, 6)
    slot = sweep(slot, 6, 7)

    def keep(g, residual):
        res_ref[group(g), :] = residual

    residuals(slot, 7, keep)

    for copy in first + second:
        copy.wait_send()
    for d in range(2):
        @pl.when(fine_has[d])
        def _():
            for t in range(EXCHANGES):
                fine_copy(t, d).wait_send()
            edge_matrix_copy(d).wait_send()

        for s in range(2 * CSWEEPS):
            @pl.when(coarse_sent(d, s % CSWEEPS == CSWEEPS - 1))
            def _():
                coarse_copy(s, d).wait_send()


def body(coarse_size, fan_size, right_side, fine_matrix, fine_columns, fine_inverse,
         prolong, aggregate, coarse_matrix, coarse_columns, coarse_inverse):
    rows, B, R = right_side.shape
    grows = coarse_matrix.shape[0]
    rc = grows // fan_size
    vmem = pl.BlockSpec(memory_space=pltpu.VMEM)
    smem = pl.BlockSpec(memory_space=pltpu.SMEM)
    flat = jax.ShapeDtypeStruct((rows * B, R), F32)
    dma = pltpu.SemaphoreType.DMA
    solution_out, residual_out = pl.pallas_call(
        functools.partial(kernel, coarse_size, fan_size),
        out_shape=(flat, flat),
        in_specs=[vmem, vmem, smem, vmem, vmem, smem, vmem, smem, vmem],
        out_specs=(vmem, vmem),
        scratch_shapes=[
            pltpu.VMEM((rows * B, 3 * H * B), BF16),
            pltpu.VMEM((rows * B, H * B), BF16),
            pltpu.VMEM((rows * B, rc * B), BF16),
            pltpu.VMEM((rc * B, rows * B), BF16),
            pltpu.VMEM((grows * B, (grows + 2 * HC) * B), BF16),
            pltpu.VMEM((grows * B, H * B), BF16),
            pltpu.VMEM((2, (rows + 2 * H) * B, 2 * R), BF16),
            pltpu.VMEM(((grows + 2 * HC) * B, 2 * R), BF16),
            pltpu.VMEM((grows * B, R), F32),
            pltpu.VMEM((2, grows * B, R), F32),
            pltpu.VMEM((EXCHANGES, 2, H * B, R), F32),
            pltpu.VMEM((EXCHANGES, 2, H * B, R), F32),
            pltpu.VMEM((2 * CSWEEPS, 2, HC * B, R), F32),
            pltpu.VMEM((2 * CSWEEPS, 2, HC * B, R), F32),
            pltpu.VMEM((2, H * B, rc * B), F32),
            pltpu.VMEM((2, H * B, rc * B), F32),
            dma((EXCHANGES, 2)),
            dma((EXCHANGES, 2)),
            dma((2, fan_size - 1)),
            dma((2, fan_size - 1)),
            dma((2 * CSWEEPS, 2)),
            dma((2 * CSWEEPS, 2)),
            dma((2,)),
            dma((2,)),
        ],
        compiler_params=pltpu.CompilerParams(
            collective_id=0, has_side_effects=True, vmem_limit_bytes=50 * 2**20),
    )(
        right_side.reshape(rows * B, R), fine_matrix, fine_columns, fine_inverse,
        prolong, aggregate, coarse_matrix, coarse_columns, coarse_inverse,
    )
    return solution_out.reshape(rows, B, R), residual_out.reshape(rows, B, R)


def solution(mesh):
    both = P(("coarse", "fan"))
    return jax.shard_map(
        functools.partial(body, mesh.shape["coarse"], mesh.shape["fan"]),
        mesh=mesh,
        in_specs=(both, both, both, both, both, both, P("coarse"), P("coarse"), P("coarse")),
        out_specs=(both, both),
        check_vma=False,
    )
```

profile of v0, /device:TPU:12, one launch (start us, length us, event | category | flops | bytes accessed | tf_op | source)
XLA Modules:
  0.0 126.7 jit_solution(14988493640933347673)
XLA Ops:
  0.6 0.8 copy.11.acol_ref
  1.4 0.0 copy-start
  1.4 1.2 copy-done
  2.6 0.0 copy-start.1
  2.6 1.0 copy-done.1
  3.6 0.0 copy-start.2
  3.6 0.9 copy-done.2
  4.6 0.0 copy-start.3
  4.6 0.9 copy-done.3
  5.5 0.0 copy-start.4
  5.5 0.9 copy-done.4
  6.4 0.0 copy-start.5
  6.4 0.7 copy-done.5
  7.1 0.0 copy-start.6
  7.1 0.7 copy-done.6
  7.8 117.4 %shard_map.104 = (f32[1024,128]{1,0:T(8,128)S(1)}, f32[1024,128]{1,0:T(8,128)S(1)}) custom-call(f32[1024,128]{1,0:T(8,128)S(1)} %bitcast.3, bf16[16,7,64,64]{3,2,1,0:T(8,128)(2,1)} %a_ref.1, s32[16,7]{1,0:T(8,128)S(1)} %copy.11.acol_ref, bf16[16,64,64]{2,1,0:T(8,128)(2,1)S(1)} %copy-done.2, bf16[16,64,64]{2,1,0:T(8,128)(2,1)S(1)} %copy-done.3, ...), custom_call_target="tpu_custom_call" | custom-call | tf_op jit(solution)/shard_map/pallas_call | solution.py:348
  125.1 0.8 copy.14
  125.9 0.8 copy.15
Async XLA Ops:
  1.4 1.2 copy-start
  2.6 1.0 copy-start.1
  3.6 0.9 copy-start.2
  4.6 0.9 copy-start.3
  5.5 0.9 copy-start.4
  6.4 0.7 copy-start.5
  7.1 0.7 copy-start.6
where the time goes:
time: 127 us
  Pallas kernels  117 us (92%)
  local copies, waits for them, and re-layouts  8.72 us (7%)
    pallas_call x1, Pallas kernels, body(): pl.pallas_call(functools.partial(kernel, coarse_size, fan_size), out_shap...  117 us
    unnamed x17, local copies, waits for them, and re-layouts  8.72 us

commit v1 on v0

v1 whole, which is shorter than its diff:
```python
import functools

import jax
import jax.numpy as jnp
from jax import lax
from jax.experimental import pallas as pl
from jax.experimental.pallas import tpu as pltpu
from jax.sharding import PartitionSpec as P

H = 4
HC = 2
CSWEEPS = 4
EXCHANGES = 8
BATCHES = 1
relaxation = 0.6
MESH = pl.DeviceIdType.MESH
F32 = jnp.float32
BF16 = jnp.bfloat16


def dot(a, b):
    return jnp.dot(a, b, preferred_element_type=F32)


def two_term(matrix, halves):
    both = dot(matrix, halves)
    width = both.shape[1] // 2
    return both[:, :width] + both[:, width:]


def pack(value):
    n = value.shape[0] // BATCHES
    return jnp.concatenate([value[i * n:(i + 1) * n] for i in range(BATCHES)], axis=1)


def unpack(value):
    w = value.shape[1] // BATCHES
    return jnp.concatenate([value[:, i * w:(i + 1) * w] for i in range(BATCHES)], axis=0)


def kernel(
    coarse_size, fan_size,
    b_ref, a_ref, acol_ref, d_ref, p_ref, agg_ref, c_ref, ccol_ref, ci_ref,
    x_ref, res_ref,
    ad, dd, pd, ptd, cd, cid, bs, xs, xhl, ehl, e_ref, rhs, edge_out, halo_in,
    ce_out, ce_in, pe_out, pe_in,
    fs_sem, fr_sem, gs_sem, gr_sem, cs_sem, cr_sem, ps_sem, pr_sem,
):
    rows, slots, B, _ = a_ref.shape
    W = b_ref.shape[1] // BATCHES
    grows = c_ref.shape[0]
    rc = grows // fan_size
    HB = H * B
    CB = HC * B
    PB = rc * B
    ng = rows // H
    c = lax.axis_index("coarse")
    f = lax.axis_index("fan")
    place = c * fan_size + f
    before, after = place - 1, place + 1
    fine_to = (
        (before // fan_size, before % fan_size),
        (after // fan_size, after % fan_size),
    )
    fine_has = (place > 0, place < coarse_size * fan_size - 1)
    coarse_to = ((c - 1, f), (c + 1, f))
    coarse_has = (c > 0, c < coarse_size - 1)
    peers = [(c, (f + k) % fan_size) for k in range(1, fan_size)]

    barrier = pltpu.get_barrier_semaphore()
    for has, to in zip(fine_has + coarse_has, fine_to + coarse_to):
        @pl.when(has)
        def _():
            pl.semaphore_signal(barrier, inc=1, device_id=to, device_id_type=MESH)
    for to in peers:
        pl.semaphore_signal(barrier, inc=1, device_id=to, device_id_type=MESH)

    half = (lax.broadcasted_iota(jnp.int32, (1, 2 * B), 1) >= B).astype(jnp.int32)

    def build(count, blocks, names, pairs, dst):
        def row(r, carry):
            doubled = []
            for block in blocks(r):
                wide = block.astype(F32)
                doubled.append(jnp.concatenate([wide, wide], axis=1))
            named = names(r)
            for p in range(pairs):
                at = half + 2 * p
                total = None
                for block, name in zip(doubled, named):
                    term = jnp.where(at == name, block, 0.0)
                    total = term if total is None else total + term
                dst[pl.ds(pl.multiple_of(r * B, B), B), 2 * p * B:(2 * p + 2) * B] = total.astype(BF16)
            return carry

        lax.fori_loop(0, count, row, 0)

    def put_halves(ref, start, value):
        high = value.astype(BF16)
        low = (value - high.astype(F32)).astype(BF16)
        n = value.shape[0]
        ref[start:start + n, :W] = high
        ref[start:start + n, W:] = low

    def group(g):
        return slice(g * HB, (g + 1) * HB)

    cg = grows // H
    last = ng - 1

    def fine_copy(h, t, d):
        return pltpu.make_async_remote_copy(
            src_ref=edge_out.at[h, t, d], dst_ref=halo_in.at[h, t, 1 - d],
            send_sem=fs_sem.at[h, t, d], recv_sem=fr_sem.at[h, t, 1 - d],
            device_id=fine_to[d], device_id_type=MESH)

    def fine_send(h, t, d, value):
        edge_out[h, t, d] = pack(value)

        @pl.when(fine_has[d])
        def _():
            fine_copy(h, t, d).start()

    def fine_wait(h, t, d, slot):
        @pl.when(fine_has[d])
        def _():
            pltpu.make_async_remote_copy(
                src_ref=edge_out.at[h, t, 1 - d], dst_ref=halo_in.at[h, t, d],
                send_sem=fs_sem.at[h, t, 1 - d], recv_sem=fr_sem.at[h, t, d],
                device_id=fine_to[d], device_id_type=MESH).wait_recv()
            put_halves(xhl.at[h, slot], d * (rows + H) * B, unpack(halo_in[h, t, d]))

    def coarse_copy(h, s, d):
        return pltpu.make_async_remote_copy(
            src_ref=ce_out.at[h, s, d], dst_ref=ce_in.at[h, s, 1 - d],
            send_sem=cs_sem.at[h, s, d], recv_sem=cr_sem.at[h, s, 1 - d],
            device_id=coarse_to[d], device_id_type=MESH)

    def coarse_sent(d, final):
        if not final:
            return coarse_has[d]
        return coarse_has[d] & (f == (fan_size - 1 if d == 0 else 0))

    def coarse_came(d, final):
        if not final:
            return coarse_has[d]
        return coarse_has[d] & (f == (0 if d == 0 else fan_size - 1))

    def coarse_send(h, s, d, value, final):
        ce_out[h, s, d] = pack(value)

        @pl.when(coarse_sent(d, final))
        def _():
            coarse_copy(h, s, d).start()

    def coarse_wait(h, s, d, final):
        @pl.when(coarse_came(d, final))
        def _():
            pltpu.make_async_remote_copy(
                src_ref=ce_out.at[h, s, 1 - d], dst_ref=ce_in.at[h, s, d],
                send_sem=cs_sem.at[h, s, 1 - d], recv_sem=cr_sem.at[h, s, d],
                device_id=coarse_to[d], device_id_type=MESH).wait_recv()
            put_halves(ehl.at[h], d * (grows + HC) * B, unpack(ce_in[h, s, d]))

    def edge_matrix_copy(d):
        return pltpu.make_async_remote_copy(
            src_ref=pe_out.at[d], dst_ref=pe_in.at[1 - d],
            send_sem=ps_sem.at[d], recv_sem=pr_sem.at[1 - d],
            device_id=fine_to[d], device_id_type=MESH)

    def gather_copy(h, cycle, k, piece):
        return pltpu.make_async_remote_copy(
            src_ref=rhs.at[h, cycle, piece], dst_ref=rhs.at[h, cycle, piece],
            send_sem=gs_sem.at[h, cycle, k], recv_sem=gr_sem.at[h, cycle, k],
            device_id=peers[k], device_id_type=MESH)

    def step_of(g, residual):
        return relaxation * dot(dd[group(g), :], residual.astype(BF16))

    def set_group(h, g, value, slot, t):
        if t is not None and g == 0:
            fine_send(h, t, 0, value)
        if t is not None and g == last:
            fine_send(h, t, 1, value)
        xs[h, group(g), :] = value
        put_halves(xhl.at[h, slot], (g + 1) * HB, value)

    def residuals(h, slot, t, use):
        def edges():
            low = bs[h, group(0), :] - two_term(ad[group(0), HB:], xhl[h, slot, HB:3 * HB, :])
            high = bs[h, group(last), :] - two_term(
                ad[group(last), :2 * HB], xhl[h, slot, last * HB:(last + 2) * HB, :])
            return low, high

        def inner():
            for g in range(1, ng - 1):
                use(g, bs[h, group(g), :] - two_term(
                    ad[group(g), :], xhl[h, slot, g * HB:(g + 3) * HB, :]))

        if t is None:
            low, high = edges()
        else:
            inner()
            low, high = edges()
            yield
            fine_wait(h, t, 0, slot)
        use(0, low - two_term(ad[group(0), :HB], xhl[h, slot, :HB, :]))
        if t is not None:
            fine_wait(h, t, 1, slot)
        use(last, high - two_term(
            ad[group(last), 2 * HB:], xhl[h, slot, (last + 2) * HB:, :]))
        if t is None:
            inner()

    def sweep(h, slot, t_in, t_out):
        def use(g, residual):
            set_group(h, g, xs[h, group(g), :] + step_of(g, residual), 1 - slot, t_out)

        yield from residuals(h, slot, t_in, use)

    def relax_coarse(values):
        return [
            relaxation * dot(cid[group(g), :], v.astype(BF16)) for g, v in enumerate(values)
        ]

    def build_prolong():
        build(rows, lambda r: [p_ref[r]], lambda r: [agg_ref[r]], rc // 2, pd)
        for g in range(ng):
            ptd[:, group(g)] = jnp.transpose(pd[group(g), :].astype(F32)).astype(BF16)

    def build_coarse():
        build(
            grows,
            lambda r: [c_ref[r, k] for k in range(c_ref.shape[1])],
            lambda r: [ccol_ref[r, k] for k in range(c_ref.shape[1])],
            (grows + 2 * HC) // 2, cd)
        build(grows, lambda r: [ci_ref[r]], lambda r: [r % H], H // 2, cid)

    def correct(h, cycle, slot, t_in):
        pieces = []
        if cycle == 0 and h == 0:
            build_prolong()

        def use(g, residual):
            pieces.append(dot(ptd[:, group(g)], residual.astype(BF16)))

        yield from residuals(h, slot, t_in, use)
        rhs[h, cycle, f] = pack(functools.reduce(jnp.add, pieces))
        for k in range(fan_size - 1):
            gather_copy(h, cycle, k, f).start()
        if cycle == 0 and h == BATCHES - 1:
            pe_out[0] = pd[:HB, :].astype(F32)
            pe_out[1] = pd[last * HB:, :].astype(F32)
            for d in range(2):
                @pl.when(fine_has[d])
                def _():
                    edge_matrix_copy(d).start()
            build_coarse()
        yield
        for k in range(fan_size - 1):
            gather_copy(h, cycle, k, (f + 2 * fan_size - k - 1) % fan_size).wait_recv()
        whole = [unpack(rhs[h, cycle, i]) for i in range(fan_size)]
        whole = jnp.concatenate(whole, axis=0)
        whole = [whole[group(g)] for g in range(cg)]
        own_rows = slice(CB, CB + grows * B)

        def publish(e, s, final):
            coarse_send(h, s, 0, e[0][:CB, :], final)
            coarse_send(h, s, 1, e[-1][HB - CB:, :], final)
            for g in range(cg):
                e_ref[h, group(g), :] = e[g]
                put_halves(ehl.at[h], CB + g * HB, e[g])

        s = cycle * CSWEEPS
        publish(relax_coarse(whole), s, False)
        for step in range(1, CSWEEPS):
            own = [
                whole[g] - two_term(cd[group(g), own_rows], ehl[h, own_rows, :])
                for g in range(cg)
            ]
            yield
            coarse_wait(h, s, 0, False)
            coarse_wait(h, s, 1, False)
            own = [v - two_term(cd[group(g), :CB], ehl[h, :CB, :]) for g, v in enumerate(own)]
            own = [
                v - two_term(cd[group(g), CB + grows * B:], ehl[h, CB + grows * B:, :])
                for g, v in enumerate(own)
            ]
            e = [e_ref[h, group(g), :] + v for g, v in enumerate(relax_coarse(own))]
            s = s + 1
            publish(e, s, step == CSWEEPS - 1)

        other = 1 - slot
        lifted = ehl[h, pl.ds(pl.multiple_of(CB + f * PB, PB), PB), :]
        for g in range(ng):
            set_group(h, g, xs[h, group(g), :] + two_term(pd[group(g), :], lifted), other, None)
        yield
        for d in range(2):
            if cycle == 0 and h == 0:
                @pl.when(fine_has[d])
                def _():
                    pltpu.make_async_remote_copy(
                        src_ref=pe_out.at[1 - d], dst_ref=pe_in.at[d],
                        send_sem=ps_sem.at[1 - d], recv_sem=pr_sem.at[d],
                        device_id=fine_to[d], device_id_type=MESH).wait_recv()
            coarse_wait(h, s, d, True)

            @pl.when(fine_has[d])
            def _():
                theirs = ehl[h, pl.ds(pl.multiple_of(CB + (f + 2 * d - 1) * PB, PB), PB), :]
                value = unpack(halo_in[h, t_in, d]) + two_term(pe_in[d].astype(BF16), theirs)
                put_halves(xhl.at[h, other], d * (rows + H) * B, value)

    build(rows, lambda r: [d_ref[r]], lambda r: [r % H], H // 2, dd)
    waits = (
        sum(h.astype(jnp.int32) for h in fine_has + coarse_has) + (fan_size - 1)
    )
    pl.semaphore_wait(barrier, waits)
    for h in range(BATCHES):
        bs[h] = b_ref[:, h * W:(h + 1) * W]
        for g in (0, last):
            set_group(h, g, step_of(g, bs[h, group(g), :]), 0, 0)
    for h in range(BATCHES):
        for g in range(1, last):
            set_group(h, g, step_of(g, bs[h, group(g), :]), 0, 0)
    for d in range(2):
        @pl.when(jnp.logical_not(fine_has[d]))
        def _():
            at = d * (rows + H) * B
            for h in range(BATCHES):
                for slot in range(2):
                    xhl[h, slot, at:at + HB, :] = jnp.zeros((HB, 2 * W), BF16)

        @pl.when(jnp.logical_not(coarse_has[d]))
        def _():
            at = d * (grows + HC) * B
            for h in range(BATCHES):
                ehl[h, at:at + CB, :] = jnp.zeros((CB, 2 * W), BF16)

    build(
        rows,
        lambda r: [a_ref[r, k] for k in range(slots)],
        lambda r: [acol_ref[r, k] - (r // H) * H for k in range(slots)],
        3 * H // 2, ad)

    def batch(h):
        def keep(g, residual):
            res_ref[group(g), h * W:(h + 1) * W] = residual

        yield from sweep(h, 0, 0, 1)
        yield from correct(h, 0, 1, 1)
        yield from sweep(h, 0, None, 2)
        yield from sweep(h, 1, 2, 3)
        yield from sweep(h, 0, 3, 4)
        yield from sweep(h, 1, 4, 5)
        yield from correct(h, 1, 0, 5)
        yield from sweep(h, 1, None, 6)
        yield from sweep(h, 0, 6, 7)
        x_ref[:, h * W:(h + 1) * W] = xs[h]
        yield from residuals(h, 1, 7, keep)

    running = [batch(h) for h in range(BATCHES)]
    while running:
        running = [one for one in running if next(one, running) is not running]

    for h in range(BATCHES):
        for cycle in range(2):
            for k in range(fan_size - 1):
                gather_copy(h, cycle, k, f).wait_send()
    for d in range(2):
        @pl.when(fine_has[d])
        def _():
            for h in range(BATCHES):
                for t in range(EXCHANGES):
                    fine_copy(h, t, d).wait_send()
            edge_matrix_copy(d).wait_send()

        for s in range(2 * CSWEEPS):
            @pl.when(coarse_sent(d, s % CSWEEPS == CSWEEPS - 1))
            def _():
                for h in range(BATCHES):
                    coarse_copy(h, s, d).wait_send()


def body(coarse_size, fan_size, right_side, fine_matrix, fine_columns, fine_inverse,
         prolong, aggregate, coarse_matrix, coarse_columns, coarse_inverse):
    rows, B, R = right_side.shape
    grows = coarse_matrix.shape[0]
    rc = grows // fan_size
    W = R // BATCHES
    vmem = pl.BlockSpec(memory_space=pltpu.VMEM)
    smem = pl.BlockSpec(memory_space=pltpu.SMEM)
    flat = jax.ShapeDtypeStruct((rows * B, R), F32)
    dma = pltpu.SemaphoreType.DMA
    solution_out, residual_out = pl.pallas_call(
        functools.partial(kernel, coarse_size, fan_size),
        out_shape=(flat, flat),
        in_specs=[vmem, vmem, smem, vmem, vmem, smem, vmem, smem, vmem],
        out_specs=(vmem, vmem),
        scratch_shapes=[
            pltpu.VMEM((rows * B, 3 * H * B), BF16),
            pltpu.VMEM((rows * B, H * B), BF16),
            pltpu.VMEM((rows * B, rc * B), BF16),
            pltpu.VMEM((rc * B, rows * B), BF16),
            pltpu.VMEM((grows * B, (grows + 2 * HC) * B), BF16),
            pltpu.VMEM((grows * B, H * B), BF16),
            pltpu.VMEM((BATCHES, rows * B, W), F32),
            pltpu.VMEM((BATCHES, rows * B, W), F32),
            pltpu.VMEM((BATCHES, 2, (rows + 2 * H) * B, 2 * W), BF16),
            pltpu.VMEM((BATCHES, (grows + 2 * HC) * B, 2 * W), BF16),
            pltpu.VMEM((BATCHES, grows * B, W), F32),
            pltpu.VMEM((BATCHES, 2, fan_size, rc * B // BATCHES, R), F32),
            pltpu.VMEM((BATCHES, EXCHANGES, 2, H * B // BATCHES, R), F32),
            pltpu.VMEM((BATCHES, EXCHANGES, 2, H * B // BATCHES, R), F32),
            pltpu.VMEM((BATCHES, 2 * CSWEEPS, 2, HC * B // BATCHES, R), F32),
            pltpu.VMEM((BATCHES, 2 * CSWEEPS, 2, HC * B // BATCHES, R), F32),
            pltpu.VMEM((2, H * B, rc * B), F32),
            pltpu.VMEM((2, H * B, rc * B), F32),
            dma((BATCHES, EXCHANGES, 2)),
            dma((BATCHES, EXCHANGES, 2)),
            dma((BATCHES, 2, fan_size - 1)),
            dma((BATCHES, 2, fan_size - 1)),
            dma((BATCHES, 2 * CSWEEPS, 2)),
            dma((BATCHES, 2 * CSWEEPS, 2)),
            dma((2,)),
            dma((2,)),
        ],
        compiler_params=pltpu.CompilerParams(
            collective_id=0, has_side_effects=True, vmem_limit_bytes=50 * 2**20),
    )(
        right_side.reshape(rows * B, R), fine_matrix, fine_columns, fine_inverse,
        prolong, aggregate, coarse_matrix, coarse_columns, coarse_inverse,
    )
    return solution_out.reshape(rows, B, R), residual_out.reshape(rows, B, R)


def solution(mesh):
    both = P(("coarse", "fan"))
    return jax.shard_map(
        functools.partial(body, mesh.shape["coarse"], mesh.shape["fan"]),
        mesh=mesh,
        in_specs=(both, both, both, both, both, both, P("coarse"), P("coarse"), P("coarse")),
        out_specs=(both, both),
        check_vma=False,
    )
```

time: 127 us -> 124 us (0.976)
  Pallas kernels: 117 us -> 114 us
    pallas_call x1, Pallas kernels: 117 us -> 114 us  [body(): pl.pallas_call(functools.partial(kernel, coarse_size, fan_size), out_shap...]
where the time goes in v1:
time: 124 us; the launch traced here: 123 us
  Pallas kernels  114 us (92%)
  local copies, waits for them, and re-layouts  8.72 us (7%)
    pallas_call x1, Pallas kernels, body(): pl.pallas_call(functools.partial(kernel, coarse_size, fan_size), out_shap...  114 us
    unnamed x17, local copies, waits for them, and re-layouts  8.72 us

profile of v1, /device:TPU:12, one launch (start us, length us, event | category | flops | bytes accessed | tf_op | source)
XLA Modules:
  0.0 123.5 jit_solution(8494555056347895144)
XLA Ops:
  0.6 0.8 copy.11.acol_ref
  1.4 0.0 copy-start
  1.4 1.2 copy-done
  2.6 0.0 copy-start.1
  2.6 1.0 copy-done.1
  3.6 0.0 copy-start.2
  3.6 0.9 copy-done.2
  4.6 0.0 copy-start.3
  4.6 0.9 copy-done.3
  5.5 0.0 copy-start.4
  5.5 0.9 copy-done.4
  6.4 0.0 copy-start.5
  6.4 0.7 copy-done.5
  7.1 0.0 copy-start.6
  7.1 0.7 copy-done.6
  7.8 114.1 %shard_map.104 = (f32[1024,128]{1,0:T(8,128)S(1)}, f32[1024,128]{1,0:T(8,128)S(1)}) custom-call(f32[1024,128]{1,0:T(8,128)S(1)} %bitcast.3, bf16[16,7,64,64]{3,2,1,0:T(8,128)(2,1)} %a_ref.1, s32[16,7]{1,0:T(8,128)S(1)} %copy.11.acol_ref, bf16[16,64,64]{2,1,0:T(8,128)(2,1)S(1)} %copy-done.2, bf16[16,64,64]{2,1,0:T(8,128)(2,1)S(1)} %copy-done.3, ...), custom_call_target="tpu_custom_call" | custom-call | tf_op jit(solution)/shard_map/pallas_call | solution.py:395
  121.9 0.8 copy.14
  122.7 0.8 copy.15
Async XLA Ops:
  1.4 1.2 copy-start
  2.6 1.0 copy-start.1
  3.6 0.9 copy-start.2
  4.6 0.9 copy-start.3
  5.5 0.9 copy-start.4
  6.4 0.7 copy-start.5
  7.1 0.7 copy-start.6
